TPU v7x, 32 devices: a whole 2x2x4 slice. The times are simulated.
32 devices in a mesh: trial: 2 (over x), tx: 4 (over y, core), ty: 4 (over z).
Axes of the slice: x: 2, y: 2, z: 4, core: 2. Of those that a mesh axis runs over, the one named last changes fastest.
Arguments:
- velocity: float32 [2, 64, 256, 128], P('trial', 'tx', 'ty'), may hold values from 1.5 to 4
- direction: float32 [2, 64, 256, 128], P('trial', 'tx', 'ty'), may hold values from -0.5 to 0.5
- wave_prev: float32 [2, 64, 256, 128], P('trial', 'tx', 'ty'), may hold values from -6 to 6
- wave_now: float32 [2, 64, 256, 128], P('trial', 'tx', 'ty'), may hold values from -5.5 to 5.5, as said below
- winner: int32 [1], replicated, may hold values from 0 to 2047
- step_lengths: float32 [2], replicated, may hold values from 0.05 to 0.5
- src_cell: int32 [1], replicated, may hold values from 0 to 2097151
- wavelet: float32 [8], replicated, may hold values from -6000 to 6000
- rec_cells: int32 [2048], replicated, may hold values from 0 to 2097151
- observed: float32 [8, 2048], replicated, may hold values from -6 to 6
Outputs:
- wave_final: float32 [2, 64, 256, 128], P('trial', 'tx', 'ty')
- misfit: float32 [2], P('trial')
Inputs may be any that keep to these rules, and one draw needn't show every extreme that they name: `wave_now`: drawn as a normal field clipped to -5 to 5, possibly with a constant offset.
All inputs are finite; a program needn't handle non-finite values.
Results may differ from a plain program's by a relative error of at most 0.0001.
Values sent between devices are 32-bit elements; how exact they have to be, the bound alone decides.
A program may use at most 64 MiB of HBM per device.

v0:
```python
import jax
import jax.numpy as jnp
from jax import lax
from jax.sharding import PartitionSpec as P

ITERS = 8
NREC = 2048


coef_mid = -2.5
coef_one = 4.0 / 3.0
coef_two = -1.0 / 12.0
dt_over_h = 0.1


def from_root(block, axis, source):
    block = jnp.where(lax.axis_index(axis) == source, block, jnp.zeros_like(block))
    return lax.psum(block, axis)


def extended(block, sides, width):
    for axis, dim in sides:
        count = lax.axis_size(axis)
        forward = [(i, i + 1) for i in range(count - 1)]
        backward = [(target, source) for source, target in forward]
        low = lax.ppermute(
            lax.slice_in_dim(block, block.shape[dim] - width, None, axis=dim), axis, forward
        )
        high = lax.ppermute(lax.slice_in_dim(block, 0, width, axis=dim), axis, backward)
        block = jnp.concatenate([low, block, high], axis=dim)
    return block


def laplace_inner(padded):
    centre = padded[2:-2, 2:-2]
    deep = jnp.pad(centre, ((0, 0), (0, 0), (2, 2)))
    total = 3.0 * coef_mid * centre
    total = total + coef_one * (padded[3:-1, 2:-2] + padded[1:-3, 2:-2])
    total = total + coef_two * (padded[4:, 2:-2] + padded[:-4, 2:-2])
    total = total + coef_one * (padded[2:-2, 3:-1] + padded[2:-2, 1:-3])
    total = total + coef_two * (padded[2:-2, 4:] + padded[2:-2, :-4])
    total = total + coef_one * (deep[:, :, 3:-1] + deep[:, :, 1:-3])
    total = total + coef_two * (deep[:, :, 4:] + deep[:, :, :-4])
    return total


def advance(prev_ext, now_pad, speed_ext, margin, amp, src_local):
    src_x, src_y, src_z = src_local
    lap = laplace_inner(now_pad)
    size_x, size_y = (lap.shape[0], lap.shape[1])
    pos_x = src_x + margin
    pos_y = src_y + margin
    inside = (pos_x >= 0) & (pos_x < size_x) & (pos_y >= 0) & (pos_y < size_y)
    lap = lap.at[jnp.clip(pos_x, 0, size_x - 1), jnp.clip(pos_y, 0, size_y - 1), src_z].add(
        jnp.where(inside, amp, 0.0)
    )
    nxt = 2.0 * now_pad[2:-2, 2:-2] - prev_ext + speed_ext * lap
    return nxt


def local(
    velocity,
    direction,
    wave_prev,
    wave_now,
    winner,
    step_lengths,
    src_cell,
    wavelet,
    rec_cells,
    observed,
):
    cells_x, cells_y, depth = (velocity.shape[1], velocity.shape[2], velocity.shape[3])
    whole_y = cells_y * lax.axis_size("ty")
    root = winner[0] % lax.axis_size("trial")
    accepted, heading = (
        from_root(velocity[0], "trial", root),
        from_root(direction[0], "trial", root),
    )
    alpha = lax.dynamic_index_in_dim(step_lengths, lax.axis_index("trial"), 0, keepdims=False)
    speed = ((accepted + alpha * heading) * dt_over_h) ** 2
    anchor_x = lax.axis_index("tx") * cells_x
    anchor_y = lax.axis_index("ty") * cells_y
    plane = whole_y * depth
    flat_src = src_cell[0]
    src_local = (
        flat_src // plane - anchor_x,
        flat_src % plane // depth - anchor_y,
        flat_src % depth,
    )
    rec_x = rec_cells // plane - anchor_x
    rec_y = rec_cells % plane // depth - anchor_y
    rec_z = rec_cells % depth
    rec_inside = (rec_x >= 0) & (rec_x < cells_x) & (rec_y >= 0) & (rec_y < cells_y)
    rec_local = (
        jnp.clip(rec_x, 0, cells_x - 1) * cells_y + jnp.clip(rec_y, 0, cells_y - 1)
    ) * depth + rec_z
    prev = wave_prev[0]
    now = wave_now[0]
    total = jnp.float32(0.0)
    for step in range(ITERS):
        padded = extended(now, (("tx", 0), ("ty", 1)), 2)
        nxt = advance(prev, padded, speed, 0, wavelet[step], src_local)
        picked = jnp.take(nxt.reshape(-1), rec_local)
        total = total + jnp.sum(jnp.where(rec_inside, (picked - observed[step]) ** 2, 0.0))
        prev, now = (now, nxt)
    summed = lax.psum(total, ("tx", "ty"))
    misfit = (summed / (ITERS * NREC)).reshape(1)
    return (now[None], misfit)


def solution(mesh):
    placed = (
        P("trial", "tx", "ty", None),
        P("trial", "tx", "ty", None),
        P("trial", "tx", "ty", None),
        P("trial", "tx", "ty", None),
        P(),
        P(),
        P(),
        P(),
        P(),
        P(),
    )
    return jax.shard_map(
        local,
        mesh=mesh,
        in_specs=placed,
        out_specs=(P("trial", "tx", "ty", None), P("trial")),
        check_vma=False,
    )
```

profile of v0, /device:TPU:0, one launch (start us, length us, event | category | flops | bytes accessed | tf_op | source)
XLA Modules:
  0.0 339.8 jit_solution(14346728913988008692)
XLA Ops:
  11.3 3.0 collective-permute-start.1
  17.8 5.6 %collective-permute-start.3 = (f32[20,2,128]{2,1,0:T(2,128)S(1)}, f32[20,2,128]{2,1,0:T(2,128)S(1)}, u32[]{:S(2)}, u32[]{:S(2)}) collective-permute-start(f32[20,2,128]{2,1,0:T(2,128)S(1)} %get-tuple-element.144), channel_id=1, source_target_pairs={{0,1},{1,2},{2,3},{4,5},{5,6},{6,7},{8,9},{9,10},{10,11},{12,13},{... | collective-permute-start | bytes 61448 | tf_op jit(solution)/shard_map/ppermute | solution.py:26
  30.2 23.7 %all-reduce.11.cloned.1.call-done = (f32[16,64,128]{2,1,0:T(8,128)}, f32[16,64,128]{2,1,0:T(8,128)}) async-done(((f32[16,64,128]{2,1,0:T(8,128)}, f32[16,64,128]{2,1,0:T(8,128)}), (f32[16,64,128]{2,1,0:T(8,128)}, f32[16,64,128]{2,1,0:T(8,128)})) %all-reduce.11.cloned.1.call-update) | async-done | bytes 1048592 | tf_op jit(solution)/shard_map/psum | solution.py:18
  62.5 4.5 %collective-permute-start.7 = (f32[20,2,128]{2,1,0:T(2,128)S(1)}, f32[20,2,128]{2,1,0:T(2,128)S(1)}, u32[]{:S(2)}, u32[]{:S(2)}) collective-permute-start(f32[20,2,128]{2,1,0:T(2,128)S(1)} %get-tuple-element.140), channel_id=1, source_target_pairs={{0,1},{1,2},{2,3},{4,5},{5,6},{6,7},{8,9},{9,10},{10,11},{12,13},{... | collective-permute-start | bytes 61448 | tf_op jit(solution)/shard_map/ppermute | solution.py:26
  78.5 4.8 %collective-permute-start.11 = (f32[20,2,128]{2,1,0:T(2,128)S(1)}, f32[20,2,128]{2,1,0:T(2,128)S(1)}, u32[]{:S(2)}, u32[]{:S(2)}) collective-permute-start(f32[20,2,128]{2,1,0:T(2,128)S(1)} %get-tuple-element.136), channel_id=1, source_target_pairs={{0,1},{1,2},{2,3},{4,5},{5,6},{6,7},{8,9},{9,10},{10,11},{12,13},{... | collective-permute-start | bytes 61448 | tf_op jit(solution)/shard_map/ppermute | solution.py:26
  89.6 5.5 %collective-permute-start.13 = (f32[2,64,128]{2,1,0:T(8,128)S(1)}, f32[2,64,128]{2,1,0:T(8,128)S(1)}, u32[]{:S(2)}, u32[]{:S(2)}) collective-permute-start(f32[2,64,128]{2,1,0:T(8,128)S(1)} %get-tuple-element.154), channel_id=1, source_target_pairs={{0,4},{4,8},{8,12},{1,5},{5,9},{9,13},{2,6},{6,10},{10,14},{3,7},{... | collective-permute-start | bytes 196616 | tf_op jit(solution)/shard_map/ppermute | solution.py:26
  97.3 4.5 %collective-permute-start.15 = (f32[20,2,128]{2,1,0:T(2,128)S(1)}, f32[20,2,128]{2,1,0:T(2,128)S(1)}, u32[]{:S(2)}, u32[]{:S(2)}) collective-permute-start(f32[20,2,128]{2,1,0:T(2,128)S(1)} %get-tuple-element.132), channel_id=1, source_target_pairs={{0,1},{1,2},{2,3},{4,5},{5,6},{6,7},{8,9},{9,10},{10,11},{12,13},{... | collective-permute-start | bytes 61448 | tf_op jit(solution)/shard_map/ppermute | solution.py:26
  108.0 5.6 %collective-permute-start.17 = (f32[2,64,128]{2,1,0:T(8,128)S(1)}, f32[2,64,128]{2,1,0:T(8,128)S(1)}, u32[]{:S(2)}, u32[]{:S(2)}) collective-permute-start(f32[2,64,128]{2,1,0:T(8,128)S(1)} %get-tuple-element.152), channel_id=1, source_target_pairs={{0,4},{4,8},{8,12},{1,5},{5,9},{9,13},{2,6},{6,10},{10,14},{3,7},{... | collective-permute-start | bytes 196616 | tf_op jit(solution)/shard_map/ppermute | solution.py:26
  115.8 4.5 %collective-permute-start.19 = (f32[20,2,128]{2,1,0:T(2,128)S(1)}, f32[20,2,128]{2,1,0:T(2,128)S(1)}, u32[]{:S(2)}, u32[]{:S(2)}) collective-permute-start(f32[20,2,128]{2,1,0:T(2,128)S(1)} %get-tuple-element.128), channel_id=1, source_target_pairs={{0,1},{1,2},{2,3},{4,5},{5,6},{6,7},{8,9},{9,10},{10,11},{12,13},{... | collective-permute-start | bytes 61448 | tf_op jit(solution)/shard_map/ppermute | solution.py:26
  130.5 5.6 %collective-permute-start.21 = (f32[2,64,128]{2,1,0:T(8,128)S(1)}, f32[2,64,128]{2,1,0:T(8,128)S(1)}, u32[]{:S(2)}, u32[]{:S(2)}) collective-permute-start(f32[2,64,128]{2,1,0:T(8,128)S(1)} %get-tuple-element.150), channel_id=1, source_target_pairs={{0,4},{4,8},{8,12},{1,5},{5,9},{9,13},{2,6},{6,10},{10,14},{3,7},{... | collective-permute-start | bytes 196616 | tf_op jit(solution)/shard_map/ppermute | solution.py:26
  138.3 4.5 %collective-permute-start.23 = (f32[20,2,128]{2,1,0:T(2,128)S(1)}, f32[20,2,128]{2,1,0:T(2,128)S(1)}, u32[]{:S(2)}, u32[]{:S(2)}) collective-permute-start(f32[20,2,128]{2,1,0:T(2,128)S(1)} %get-tuple-element.124), channel_id=1, source_target_pairs={{0,1},{1,2},{2,3},{4,5},{5,6},{6,7},{8,9},{9,10},{10,11},{12,13},{... | collective-permute-start | bytes 61448 | tf_op jit(solution)/shard_map/ppermute | solution.py:26
  153.1 5.6 %collective-permute-start.25 = (f32[2,64,128]{2,1,0:T(8,128)S(1)}, f32[2,64,128]{2,1,0:T(8,128)S(1)}, u32[]{:S(2)}, u32[]{:S(2)}) collective-permute-start(f32[2,64,128]{2,1,0:T(8,128)S(1)} %get-tuple-element.148), channel_id=1, source_target_pairs={{0,4},{4,8},{8,12},{1,5},{5,9},{9,13},{2,6},{6,10},{10,14},{3,7},{... | collective-permute-start | bytes 196616 | tf_op jit(solution)/shard_map/ppermute | solution.py:26
  160.9 4.5 %collective-permute-start.27 = (f32[20,2,128]{2,1,0:T(2,128)S(1)}, f32[20,2,128]{2,1,0:T(2,128)S(1)}, u32[]{:S(2)}, u32[]{:S(2)}) collective-permute-start(f32[20,2,128]{2,1,0:T(2,128)S(1)} %get-tuple-element.120), channel_id=1, source_target_pairs={{0,1},{1,2},{2,3},{4,5},{5,6},{6,7},{8,9},{9,10},{10,11},{12,13},{... | collective-permute-start | bytes 61448 | tf_op jit(solution)/shard_map/ppermute | solution.py:26
  175.2 5.6 %collective-permute-start.29 = (f32[2,64,128]{2,1,0:T(8,128)S(1)}, f32[2,64,128]{2,1,0:T(8,128)S(1)}, u32[]{:S(2)}, u32[]{:S(2)}) collective-permute-start(f32[2,64,128]{2,1,0:T(8,128)S(1)} %get-tuple-element.146), channel_id=1, source_target_pairs={{0,4},{4,8},{8,12},{1,5},{5,9},{9,13},{2,6},{6,10},{10,14},{3,7},{... | collective-permute-start | bytes 196616 | tf_op jit(solution)/shard_map/ppermute | solution.py:26
  183.0 4.7 %collective-permute-start.31 = (f32[20,2,128]{2,1,0:T(2,128)S(1)}, f32[20,2,128]{2,1,0:T(2,128)S(1)}, u32[]{:S(2)}, u32[]{:S(2)}) collective-permute-start(f32[20,2,128]{2,1,0:T(2,128)S(1)} %get-tuple-element.116), channel_id=1, source_target_pairs={{0,1},{1,2},{2,3},{4,5},{5,6},{6,7},{8,9},{9,10},{10,11},{12,13},{... | collective-permute-start | bytes 61448 | tf_op jit(solution)/shard_map/ppermute | solution.py:26
  188.4 11.8 %gather_fusion = f32[2048]{0:T(1024)S(1)} fusion(f32[131072]{0:T(1024)S(1)} %bitcast.63, s32[2048]{0:T(1024)S(1)} %get-tuple-element.109), kind=kCustom, calls=%fused_computation.clone | custom fusion | bytes 24576 | tf_op jit(solution)/shard_map/jit(_take)/gather | solution.py:104
  200.2 11.8 %gather_fusion.1 = f32[2048]{0:T(1024)S(1)} fusion(f32[131072]{0:T(1024)S(1)} %bitcast.64, s32[2048]{0:T(1024)S(1)} %get-tuple-element.109), kind=kCustom, calls=%fused_computation.1.clone | custom fusion | bytes 24576 | tf_op jit(solution)/shard_map/jit(_take)/gather | solution.py:104
  212.0 11.8 %gather_fusion.2 = f32[2048]{0:T(1024)S(1)} fusion(f32[131072]{0:T(1024)S(1)} %bitcast.65, s32[2048]{0:T(1024)S(1)} %get-tuple-element.109), kind=kCustom, calls=%fused_computation.2.clone | custom fusion | bytes 24576 | tf_op jit(solution)/shard_map/jit(_take)/gather | solution.py:104
  223.8 11.8 %gather_fusion.3 = f32[2048]{0:T(1024)S(1)} fusion(f32[131072]{0:T(1024)S(1)} %bitcast.66, s32[2048]{0:T(1024)S(1)} %get-tuple-element.109), kind=kCustom, calls=%fused_computation.3.clone | custom fusion | bytes 24576 | tf_op jit(solution)/shard_map/jit(_take)/gather | solution.py:104
  235.6 11.8 %gather_fusion.4 = f32[2048]{0:T(1024)S(1)} fusion(f32[131072]{0:T(1024)S(1)} %bitcast.67, s32[2048]{0:T(1024)S(1)} %get-tuple-element.109), kind=kCustom, calls=%fused_computation.4.clone | custom fusion | bytes 24576 | tf_op jit(solution)/shard_map/jit(_take)/gather | solution.py:104
  247.4 11.8 %gather_fusion.5 = f32[2048]{0:T(1024)S(1)} fusion(f32[131072]{0:T(1024)S(1)} %bitcast.68, s32[2048]{0:T(1024)S(1)} %get-tuple-element.109), kind=kCustom, calls=%fused_computation.5.clone | custom fusion | bytes 24576 | tf_op jit(solution)/shard_map/jit(_take)/gather | solution.py:104
  259.2 11.8 %gather_fusion.6 = f32[2048]{0:T(1024)S(1)} fusion(f32[131072]{0:T(1024)S(1)} %bitcast.69, s32[2048]{0:T(1024)S(1)} %get-tuple-element.109), kind=kCustom, calls=%fused_computation.6.clone | custom fusion | bytes 24576 | tf_op jit(solution)/shard_map/jit(_take)/gather | solution.py:104
  278.3 11.8 %gather_fusion.7 = f32[2048]{0:T(1024)S(1)} fusion(f32[131072]{0:T(1024)S(1)} %bitcast.70, s32[2048]{0:T(1024)S(1)} %get-tuple-element.109), kind=kCustom, calls=%fused_computation.7.clone | custom fusion | bytes 24576 | tf_op jit(solution)/shard_map/jit(_take)/gather | solution.py:104
  295.7 35.5 %psum.23 = f32[]{:T(128)} all-reduce(f32[]{:T(128)S(6)} %add.608), channel_id=1, replica_groups=mesh['trial'=2,'tx'=4,'ty'=4] {'tx','ty'}, use_global_device_ids=true, to_apply=%region_11.13 | all-reduce | flops 1 | bytes 8 | tf_op jit(solution)/shard_map/psum | solution.py:107
  (141 shorter events, 74.5 us)
Async XLA Ops:
  7.2 46.7 %all-reduce.11.cloned.1.call-start = ((), (), s32[]{:S(2)}) async-start(), calls=%async_computation | async-start | bytes 2097152 | tf_op jit(solution)/shard_map/psum | solution.py:18
  10.0 6.4 %collective-permute-start = (f32[2,64,128]{2,1,0:T(8,128)S(1)}, f32[2,64,128]{2,1,0:T(8,128)S(1)}, u32[]{:S(2)}, u32[]{:S(2)}) collective-permute-start(f32[2,64,128]{2,1,0:T(8,128)S(1)} %get-tuple-element.159), channel_id=1, source_target_pairs={{4,0},{8,4},{12,8},{5,1},{9,5},{13,9},{6,2},{10,6},{14,10},{7,3},{... | collective-permute-start | bytes 196616 | tf_op jit(solution)/shard_map/ppermute | solution.py:29
  16.5 10.2 %collective-permute-start.2 = (f32[20,2,128]{2,1,0:T(2,128)S(1)}, f32[20,2,128]{2,1,0:T(2,128)S(1)}, u32[]{:S(2)}, u32[]{:S(2)}) collective-permute-start(f32[20,2,128]{2,1,0:T(2,128)S(1)} %get-tuple-element.143), channel_id=1, source_target_pairs={{1,0},{2,1},{3,2},{5,4},{6,5},{7,6},{9,8},{10,9},{11,10},{13,12},{... | collective-permute-start | bytes 61448 | tf_op jit(solution)/shard_map/ppermute | solution.py:29
  17.8 8.9 %collective-permute-start.3 = (f32[20,2,128]{2,1,0:T(2,128)S(1)}, f32[20,2,128]{2,1,0:T(2,128)S(1)}, u32[]{:S(2)}, u32[]{:S(2)}) collective-permute-start(f32[20,2,128]{2,1,0:T(2,128)S(1)} %get-tuple-element.144), channel_id=1, source_target_pairs={{0,1},{1,2},{2,3},{4,5},{5,6},{6,7},{8,9},{9,10},{10,11},{12,13},{... | collective-permute-start | bytes 61448 | tf_op jit(solution)/shard_map/ppermute | solution.py:26
  61.2 6.5 %collective-permute-start.6 = (f32[20,2,128]{2,1,0:T(2,128)S(1)}, f32[20,2,128]{2,1,0:T(2,128)S(1)}, u32[]{:S(2)}, u32[]{:S(2)}) collective-permute-start(f32[20,2,128]{2,1,0:T(2,128)S(1)} %get-tuple-element.139), channel_id=1, source_target_pairs={{1,0},{2,1},{3,2},{5,4},{6,5},{7,6},{9,8},{10,9},{11,10},{13,12},{... | collective-permute-start | bytes 61448 | tf_op jit(solution)/shard_map/ppermute | solution.py:29
  62.5 6.0 %collective-permute-start.7 = (f32[20,2,128]{2,1,0:T(2,128)S(1)}, f32[20,2,128]{2,1,0:T(2,128)S(1)}, u32[]{:S(2)}, u32[]{:S(2)}) collective-permute-start(f32[20,2,128]{2,1,0:T(2,128)S(1)} %get-tuple-element.140), channel_id=1, source_target_pairs={{0,1},{1,2},{2,3},{4,5},{5,6},{6,7},{8,9},{9,10},{10,11},{12,13},{... | collective-permute-start | bytes 61448 | tf_op jit(solution)/shard_map/ppermute | solution.py:26
  77.2 6.8 %collective-permute-start.10 = (f32[20,2,128]{2,1,0:T(2,128)S(1)}, f32[20,2,128]{2,1,0:T(2,128)S(1)}, u32[]{:S(2)}, u32[]{:S(2)}) collective-permute-start(f32[20,2,128]{2,1,0:T(2,128)S(1)} %get-tuple-element.135), channel_id=1, source_target_pairs={{1,0},{2,1},{3,2},{5,4},{6,5},{7,6},{9,8},{10,9},{11,10},{13,12},{... | collective-permute-start | bytes 61448 | tf_op jit(solution)/shard_map/ppermute | solution.py:29
  78.5 6.3 %collective-permute-start.11 = (f32[20,2,128]{2,1,0:T(2,128)S(1)}, f32[20,2,128]{2,1,0:T(2,128)S(1)}, u32[]{:S(2)}, u32[]{:S(2)}) collective-permute-start(f32[20,2,128]{2,1,0:T(2,128)S(1)} %get-tuple-element.136), channel_id=1, source_target_pairs={{0,1},{1,2},{2,3},{4,5},{5,6},{6,7},{8,9},{9,10},{10,11},{12,13},{... | collective-permute-start | bytes 61448 | tf_op jit(solution)/shard_map/ppermute | solution.py:26
  88.3 6.8 %collective-permute-start.12 = (f32[2,64,128]{2,1,0:T(8,128)S(1)}, f32[2,64,128]{2,1,0:T(8,128)S(1)}, u32[]{:S(2)}, u32[]{:S(2)}) collective-permute-start(f32[2,64,128]{2,1,0:T(8,128)S(1)} %get-tuple-element.153), channel_id=1, source_target_pairs={{4,0},{8,4},{12,8},{5,1},{9,5},{13,9},{6,2},{10,6},{14,10},{7,3},{... | collective-permute-start | bytes 196616 | tf_op jit(solution)/shard_map/ppermute | solution.py:29
  89.6 6.4 %collective-permute-start.13 = (f32[2,64,128]{2,1,0:T(8,128)S(1)}, f32[2,64,128]{2,1,0:T(8,128)S(1)}, u32[]{:S(2)}, u32[]{:S(2)}) collective-permute-start(f32[2,64,128]{2,1,0:T(8,128)S(1)} %get-tuple-element.154), channel_id=1, source_target_pairs={{0,4},{4,8},{8,12},{1,5},{5,9},{9,13},{2,6},{6,10},{10,14},{3,7},{... | collective-permute-start | bytes 196616 | tf_op jit(solution)/shard_map/ppermute | solution.py:26
  96.0 6.5 %collective-permute-start.14 = (f32[20,2,128]{2,1,0:T(2,128)S(1)}, f32[20,2,128]{2,1,0:T(2,128)S(1)}, u32[]{:S(2)}, u32[]{:S(2)}) collective-permute-start(f32[20,2,128]{2,1,0:T(2,128)S(1)} %get-tuple-element.131), channel_id=1, source_target_pairs={{1,0},{2,1},{3,2},{5,4},{6,5},{7,6},{9,8},{10,9},{11,10},{13,12},{... | collective-permute-start | bytes 61448 | tf_op jit(solution)/shard_map/ppermute | solution.py:29
  106.7 6.9 %collective-permute-start.16 = (f32[2,64,128]{2,1,0:T(8,128)S(1)}, f32[2,64,128]{2,1,0:T(8,128)S(1)}, u32[]{:S(2)}, u32[]{:S(2)}) collective-permute-start(f32[2,64,128]{2,1,0:T(8,128)S(1)} %get-tuple-element.151), channel_id=1, source_target_pairs={{4,0},{8,4},{12,8},{5,1},{9,5},{13,9},{6,2},{10,6},{14,10},{7,3},{... | collective-permute-start | bytes 196616 | tf_op jit(solution)/shard_map/ppermute | solution.py:29
  108.0 6.5 %collective-permute-start.17 = (f32[2,64,128]{2,1,0:T(8,128)S(1)}, f32[2,64,128]{2,1,0:T(8,128)S(1)}, u32[]{:S(2)}, u32[]{:S(2)}) collective-permute-start(f32[2,64,128]{2,1,0:T(8,128)S(1)} %get-tuple-element.152), channel_id=1, source_target_pairs={{0,4},{4,8},{8,12},{1,5},{5,9},{9,13},{2,6},{6,10},{10,14},{3,7},{... | collective-permute-start | bytes 196616 | tf_op jit(solution)/shard_map/ppermute | solution.py:26
  114.5 6.5 %collective-permute-start.18 = (f32[20,2,128]{2,1,0:T(2,128)S(1)}, f32[20,2,128]{2,1,0:T(2,128)S(1)}, u32[]{:S(2)}, u32[]{:S(2)}) collective-permute-start(f32[20,2,128]{2,1,0:T(2,128)S(1)} %get-tuple-element.127), channel_id=1, source_target_pairs={{1,0},{2,1},{3,2},{5,4},{6,5},{7,6},{9,8},{10,9},{11,10},{13,12},{... | collective-permute-start | bytes 61448 | tf_op jit(solution)/shard_map/ppermute | solution.py:29
  129.2 6.9 %collective-permute-start.20 = (f32[2,64,128]{2,1,0:T(8,128)S(1)}, f32[2,64,128]{2,1,0:T(8,128)S(1)}, u32[]{:S(2)}, u32[]{:S(2)}) collective-permute-start(f32[2,64,128]{2,1,0:T(8,128)S(1)} %get-tuple-element.149), channel_id=1, source_target_pairs={{4,0},{8,4},{12,8},{5,1},{9,5},{13,9},{6,2},{10,6},{14,10},{7,3},{... | collective-permute-start | bytes 196616 | tf_op jit(solution)/shard_map/ppermute | solution.py:29
  130.5 6.5 %collective-permute-start.21 = (f32[2,64,128]{2,1,0:T(8,128)S(1)}, f32[2,64,128]{2,1,0:T(8,128)S(1)}, u32[]{:S(2)}, u32[]{:S(2)}) collective-permute-start(f32[2,64,128]{2,1,0:T(8,128)S(1)} %get-tuple-element.150), channel_id=1, source_target_pairs={{0,4},{4,8},{8,12},{1,5},{5,9},{9,13},{2,6},{6,10},{10,14},{3,7},{... | collective-permute-start | bytes 196616 | tf_op jit(solution)/shard_map/ppermute | solution.py:26
  137.0 6.4 %collective-permute-start.22 = (f32[20,2,128]{2,1,0:T(2,128)S(1)}, f32[20,2,128]{2,1,0:T(2,128)S(1)}, u32[]{:S(2)}, u32[]{:S(2)}) collective-permute-start(f32[20,2,128]{2,1,0:T(2,128)S(1)} %get-tuple-element.123), channel_id=1, source_target_pairs={{1,0},{2,1},{3,2},{5,4},{6,5},{7,6},{9,8},{10,9},{11,10},{13,12},{... | collective-permute-start | bytes 61448 | tf_op jit(solution)/shard_map/ppermute | solution.py:29
  151.8 6.9 %collective-permute-start.24 = (f32[2,64,128]{2,1,0:T(8,128)S(1)}, f32[2,64,128]{2,1,0:T(8,128)S(1)}, u32[]{:S(2)}, u32[]{:S(2)}) collective-permute-start(f32[2,64,128]{2,1,0:T(8,128)S(1)} %get-tuple-element.147), channel_id=1, source_target_pairs={{4,0},{8,4},{12,8},{5,1},{9,5},{13,9},{6,2},{10,6},{14,10},{7,3},{... | collective-permute-start | bytes 196616 | tf_op jit(solution)/shard_map/ppermute | solution.py:29
  153.1 6.5 %collective-permute-start.25 = (f32[2,64,128]{2,1,0:T(8,128)S(1)}, f32[2,64,128]{2,1,0:T(8,128)S(1)}, u32[]{:S(2)}, u32[]{:S(2)}) collective-permute-start(f32[2,64,128]{2,1,0:T(8,128)S(1)} %get-tuple-element.148), channel_id=1, source_target_pairs={{0,4},{4,8},{8,12},{1,5},{5,9},{9,13},{2,6},{6,10},{10,14},{3,7},{... | collective-permute-start | bytes 196616 | tf_op jit(solution)/shard_map/ppermute | solution.py:26
  159.6 6.5 %collective-permute-start.26 = (f32[20,2,128]{2,1,0:T(2,128)S(1)}, f32[20,2,128]{2,1,0:T(2,128)S(1)}, u32[]{:S(2)}, u32[]{:S(2)}) collective-permute-start(f32[20,2,128]{2,1,0:T(2,128)S(1)} %get-tuple-element.119), channel_id=1, source_target_pairs={{1,0},{2,1},{3,2},{5,4},{6,5},{7,6},{9,8},{10,9},{11,10},{13,12},{... | collective-permute-start | bytes 61448 | tf_op jit(solution)/shard_map/ppermute | solution.py:29
  173.8 7.1 %collective-permute-start.28 = (f32[2,64,128]{2,1,0:T(8,128)S(1)}, f32[2,64,128]{2,1,0:T(8,128)S(1)}, u32[]{:S(2)}, u32[]{:S(2)}) collective-permute-start(f32[2,64,128]{2,1,0:T(8,128)S(1)} %get-tuple-element.145), channel_id=1, source_target_pairs={{4,0},{8,4},{12,8},{5,1},{9,5},{13,9},{6,2},{10,6},{14,10},{7,3},{... | collective-permute-start | bytes 196616 | tf_op jit(solution)/shard_map/ppermute | solution.py:29
  175.2 6.5 %collective-permute-start.29 = (f32[2,64,128]{2,1,0:T(8,128)S(1)}, f32[2,64,128]{2,1,0:T(8,128)S(1)}, u32[]{:S(2)}, u32[]{:S(2)}) collective-permute-start(f32[2,64,128]{2,1,0:T(8,128)S(1)} %get-tuple-element.146), channel_id=1, source_target_pairs={{0,4},{4,8},{8,12},{1,5},{5,9},{9,13},{2,6},{6,10},{10,14},{3,7},{... | collective-permute-start | bytes 196616 | tf_op jit(solution)/shard_map/ppermute | solution.py:26
  181.7 89.2 %collective-permute-start.30 = (f32[20,2,128]{2,1,0:T(2,128)S(1)}, f32[20,2,128]{2,1,0:T(2,128)S(1)}, u32[]{:S(2)}, u32[]{:S(2)}) collective-permute-start(f32[20,2,128]{2,1,0:T(2,128)S(1)} %get-tuple-element.115), channel_id=1, source_target_pairs={{1,0},{2,1},{3,2},{5,4},{6,5},{7,6},{9,8},{10,9},{11,10},{13,12},{... | collective-permute-start | bytes 61448 | tf_op jit(solution)/shard_map/ppermute | solution.py:29
  183.0 87.9 %collective-permute-start.31 = (f32[20,2,128]{2,1,0:T(2,128)S(1)}, f32[20,2,128]{2,1,0:T(2,128)S(1)}, u32[]{:S(2)}, u32[]{:S(2)}) collective-permute-start(f32[20,2,128]{2,1,0:T(2,128)S(1)} %get-tuple-element.116), channel_id=1, source_target_pairs={{0,1},{1,2},{2,3},{4,5},{5,6},{6,7},{8,9},{9,10},{10,11},{12,13},{... | collective-permute-start | bytes 61448 | tf_op jit(solution)/shard_map/ppermute | solution.py:26
  (22 other events, 199.4 us)
Sparse Core Ops, SparseCore 0:
  10.9 42.9 all-reduce.10
where the time goes:
time: 342 us; the launch traced here: 340 us
  local copies, waits for them, and re-layouts  112 us (33%)
  starting transfers between devices  95.8 us (28%)
  between operations  43 us (13%)
  blocking collectives  35.5 us (10%)
  waiting for transfers between devices  34.7 us (10%)
  other arithmetic  18.6 us (5%)
    gather x8, local copies, waits for them, and re-layouts, local(): picked = jnp.take(nxt.reshape(-1), rec_local)  94.3 us
    ppermute x16, starting transfers between devices, extended(): lax.ppermute(lax.slice_in_dim(block, block.shape[dim] - width, None, axis...  74.9 us
    psum x1, blocking collectives, local(): summed = lax.psum(total, ('tx', 'ty'))  35.5 us
    psum x1, waiting for transfers between devices, from_root(): return lax.psum(block, axis)  23.7 us
    ppermute x16, starting transfers between devices, extended(): lax.ppermute(lax.slice_in_dim(block, 0, width, axis=dim), axis, backward)  20.8 us
    ppermute x16, waiting for transfers between devices, extended(): lax.ppermute(lax.slice_in_dim(block, block.shape[dim] - width, None, axis...  11 us
    add x8, other arithmetic, advance(): nxt = 2.0 * now_pad[2:-2, 2:-2] - prev_ext + speed_ext * lap  7.71 us
    add x8, other arithmetic, laplace_inner(): total = total + coef_two * (deep[:, :, 4:] + deep[:, :, :-4])  7.29 us
  transfers between devices with their start and end apart: 33, of which 14 were waited for; matrix products, arithmetic and copies ran while one was open for 25% of the time, Pallas kernels for 0%

commit v1 on v0

v1 whole, which is shorter than its diff:
```python
import functools

import jax
import jax.numpy as jnp
from jax import lax
from jax.experimental import pallas as pl
from jax.experimental.pallas import tpu as pltpu
from jax.sharding import PartitionSpec as P

MESH = pl.DeviceIdType.MESH
coef_mid = -2.5
coef_one = 4.0 / 3.0
coef_two = -1.0 / 12.0
dt_over_h = 0.1
HALO = 2
PAD = 8
CHUNK = 256


def from_root(block, axis, source):
    block = jnp.where(lax.axis_index(axis) == source, block, jnp.zeros_like(block))
    return lax.psum(block, axis)


def kernel(
    sizes,
    vel_ref,
    dir_ref,
    prev_ref,
    now_ref,
    winner_ref,
    steps_ref,
    src_ref,
    wavelet_ref,
    recrow_ref,
    recz_ref,
    obs_ref,
    out_ref,
    misfit_ref,
    field,
    speed,
    speed_out,
    speed_in,
    y_out,
    y_in,
    hot,
    lhs,
    acc,
    red,
    x_send,
    x_recv,
    y_send,
    y_recv,
    sp_send,
    sp_recv,
    red_send,
    red_recv,
):
    trials, tiles_x, tiles_y = sizes
    cells_x, cells_y, depth = now_ref.shape[1:]
    iters, nrec = obs_ref.shape
    exchange = trials == 2
    k = lax.axis_index("trial")
    ix = lax.axis_index("tx")
    iy = lax.axis_index("ty")
    inner_x = pl.ds(HALO, cells_x)
    inner_y = pl.ds(PAD, cells_y)

    for slot in range(2):
        for x in (0, 1, HALO + cells_x, HALO + cells_x + 1):
            field[slot, x] = jnp.zeros(field.shape[2:], jnp.float32)
        field[slot, inner_x, pl.ds(0, PAD)] = jnp.zeros((cells_x, PAD, depth), jnp.float32)
        field[slot, inner_x, pl.ds(PAD + cells_y, PAD)] = jnp.zeros(
            (cells_x, PAD, depth), jnp.float32
        )

    barrier = pltpu.get_barrier_semaphore()
    greeted = 0
    for d in range(1, tiles_x):
        pl.semaphore_signal(
            barrier, inc=1, device_id={"tx": lax.rem(ix + d, tiles_x)}, device_id_type=MESH
        )
        greeted += 1
    for d in range(1, tiles_y):
        pl.semaphore_signal(
            barrier, inc=1, device_id={"ty": lax.rem(iy + d, tiles_y)}, device_id_type=MESH
        )
        greeted += 1
    if exchange:
        pl.semaphore_signal(barrier, inc=1, device_id={"trial": 1 - k}, device_id_type=MESH)
        greeted += 1

    mine = steps_ref[k]
    if exchange:
        other = steps_ref[1 - k]

    def speeds(x, _):
        v = vel_ref[0, x]
        d = dir_ref[0, x]
        own = (v + mine * d) * dt_over_h
        speed[x] = own * own
        if exchange:
            far = (v + other * d) * dt_over_h
            speed_out[x] = far * far
        field[0, HALO + x, inner_y] = now_ref[0, x]
        field[1, HALO + x, inner_y] = prev_ref[0, x]
        return 0

    lax.fori_loop(0, cells_x, speeds, 0)
    if greeted:
        pl.semaphore_wait(barrier, greeted)

    def x_copy(slot, side):
        src = HALO if side == 0 else cells_x
        dst = HALO + cells_x if side == 0 else 0
        to = jnp.maximum(ix - 1, 0) if side == 0 else jnp.minimum(ix + 1, tiles_x - 1)
        return pltpu.make_async_remote_copy(
            src_ref=field.at[slot, pl.ds(src, HALO), inner_y],
            dst_ref=field.at[slot, pl.ds(dst, HALO), inner_y],
            send_sem=x_send.at[slot, side],
            recv_sem=x_recv.at[slot, side],
            device_id={"tx": to},
            device_id_type=MESH,
        )

    def y_copy(slot, side):
        to = jnp.maximum(iy - 1, 0) if side == 0 else jnp.minimum(iy + 1, tiles_y - 1)
        return pltpu.make_async_remote_copy(
            src_ref=y_out.at[slot, side],
            dst_ref=y_in.at[slot, side],
            send_sem=y_send.at[slot, side],
            recv_sem=y_recv.at[slot, side],
            device_id={"ty": to},
            device_id_type=MESH,
        )

    below_x, above_x = ix > 0, ix < tiles_x - 1
    below_y, above_y = iy > 0, iy < tiles_y - 1

    def send_faces(slot):
        @pl.when(below_x)
        def _():
            x_copy(slot, 0).start()

        @pl.when(above_x)
        def _():
            x_copy(slot, 1).start()

        for j in range(HALO):
            y_out[slot, 0, j] = field[slot, inner_x, PAD + j, :]
            y_out[slot, 1, j] = field[slot, inner_x, PAD + cells_y - HALO + j, :]

        @pl.when(below_y)
        def _():
            y_copy(slot, 0).start()

        @pl.when(above_y)
        def _():
            y_copy(slot, 1).start()

    def take_faces(slot):
        @pl.when(below_x)
        def _():
            x_copy(slot, 1).wait_recv()
            x_copy(slot, 0).wait_send()

        @pl.when(above_x)
        def _():
            x_copy(slot, 0).wait_recv()
            x_copy(slot, 1).wait_send()

        @pl.when(below_y)
        def _():
            y_copy(slot, 1).wait_recv()
            y_copy(slot, 0).wait_send()
            for j in range(HALO):
                field[slot, inner_x, PAD - HALO + j, :] = y_in[slot, 1, j]

        @pl.when(above_y)
        def _():
            y_copy(slot, 0).wait_recv()
            y_copy(slot, 1).wait_send()
            for j in range(HALO):
                field[slot, inner_x, PAD + cells_y + j, :] = y_in[slot, 0, j]

    send_faces(0)
    if exchange:
        speed_copy = pltpu.make_async_remote_copy(
            src_ref=speed_out,
            dst_ref=speed_in,
            send_sem=sp_send,
            recv_sem=sp_recv,
            device_id={"trial": 1 - k},
            device_id_type=MESH,
        )
        speed_copy.start()

    rows = cells_x * cells_y
    step_rows = 256 if rows % 256 == 0 else rows
    for c in range(nrec // CHUNK):
        at = recrow_ref[:, c * CHUNK : (c + 1) * CHUNK]

        def mark(b, _, c=c, at=at):
            row = lax.broadcasted_iota(jnp.int32, (step_rows, CHUNK), 0) + b * step_rows
            start = pl.multiple_of(b * step_rows, step_rows)
            hot[c, pl.ds(start, step_rows)] = jnp.where(row == at, 1.0, 0.0).astype(jnp.bfloat16)
            return 0

        lax.fori_loop(0, rows // step_rows, mark, 0)
    acc[...] = jnp.zeros_like(acc)

    whole_y = cells_y * tiles_y
    flat = src_ref[0]
    src_x = lax.div(flat, whole_y * depth) - ix * cells_x
    in_plane = lax.rem(flat, whole_y * depth)
    src_y = lax.div(in_plane, depth) - iy * cells_y
    src_yz = jnp.where(
        (src_y >= 0) & (src_y < cells_y), src_y * depth + lax.rem(in_plane, depth), -1
    )

    plane = (cells_y, depth)
    lane = lax.broadcasted_iota(jnp.int32, (1, depth), 1)
    up1 = jnp.where(lane >= 1, coef_one, 0.0).astype(jnp.float32)
    up2 = jnp.where(lane >= 2, coef_two, 0.0).astype(jnp.float32)
    dn1 = jnp.where(lane < depth - 1, coef_one, 0.0).astype(jnp.float32)
    dn2 = jnp.where(lane < depth - 2, coef_two, 0.0).astype(jnp.float32)

    if exchange:
        speed_copy.wait()
        who = jnp.full(plane, lax.rem(winner_ref[0], trials), jnp.int32)
        keep = who == k

        def choose(x, _):
            speed[x] = jnp.where(keep, speed[x], speed_in[x])
            return 0

        lax.fori_loop(0, cells_x, choose, 0)

    def step(t, _):
        slot = lax.rem(t, 2)
        late = 1 - slot
        take_faces(slot)
        amp = wavelet_ref[t]

        def advance(x, _):
            u = field[slot, x + HALO, inner_y]
            total = (3.0 * coef_mid) * u
            near = field[slot, x + 3, inner_y] + field[slot, x + 1, inner_y]
            far = field[slot, x + 4, inner_y] + field[slot, x, inner_y]
            near = near + (
                field[slot, x + HALO, pl.ds(PAD + 1, cells_y)]
                + field[slot, x + HALO, pl.ds(PAD - 1, cells_y)]
            )
            far = far + (
                field[slot, x + HALO, pl.ds(PAD + 2, cells_y)]
                + field[slot, x + HALO, pl.ds(PAD - 2, cells_y)]
            )
            total = total + coef_one * near + coef_two * far
            total = total + up1 * pltpu.roll(u, 1, 1) + dn1 * pltpu.roll(u, depth - 1, 1)
            total = total + up2 * pltpu.roll(u, 2, 1) + dn2 * pltpu.roll(u, depth - 2, 1)
            place = lax.broadcasted_iota(jnp.int32, plane, 0) * depth
            place = place + lax.broadcasted_iota(jnp.int32, plane, 1)
            here = jnp.where(src_x == x, src_yz, -1)
            total = total + jnp.where(place == here, amp, 0.0)
            prev = field[late, x + HALO, inner_y]
            field[late, x + HALO, inner_y] = 2.0 * u - prev + speed[x] * total
            return 0

        lax.fori_loop(0, cells_x, advance, 0)

        @pl.when(t < iters - 1)
        def _():
            send_faces(late)

        pair = max(1, 128 // cells_y)
        wide = pair * cells_y
        for p in range(cells_x // pair):
            block = field[late, pl.ds(HALO + p * pair, pair), inner_y]
            turned = block.reshape(wide, depth).T
            high = turned.astype(jnp.bfloat16)
            left = turned - high.astype(jnp.float32)
            middle = left.astype(jnp.bfloat16)
            low = (left - middle.astype(jnp.float32)).astype(jnp.bfloat16)
            lhs[0:depth, p * wide : (p + 1) * wide] = high
            lhs[depth : 2 * depth, p * wide : (p + 1) * wide] = middle
            lhs[2 * depth : 3 * depth, p * wide : (p + 1) * wide] = low
        zs = lax.broadcasted_iota(jnp.int32, (depth, CHUNK), 0)
        for c in range(nrec // CHUNK):
            got = jnp.dot(lhs[...], hot[c], preferred_element_type=jnp.float32)
            picked = got[:depth] + (got[depth : 2 * depth] + got[2 * depth :])
            cols = pl.ds(c * CHUNK, CHUNK)
            gap = picked - obs_ref[pl.ds(t, 1), cols]
            part = jnp.where(zs == recz_ref[:, cols], gap * gap, 0.0)
            part = part.reshape(depth // 8, 8, CHUNK).sum(axis=0)
            acc[...] += part[:, :128] + part[:, 128:]
        return 0

    lax.fori_loop(0, iters, step, 0)

    for phase, (axis, me, count) in enumerate((("tx", ix, tiles_x), ("ty", iy, tiles_y))):
        red[phase, 0] = acc[...]
        copies = []
        for d in range(1, count):
            copy = pltpu.make_async_remote_copy(
                src_ref=red.at[phase, 0],
                dst_ref=red.at[phase, d],
                send_sem=red_send.at[phase, d],
                recv_sem=red_recv.at[phase, d],
                device_id={axis: lax.rem(me + d, count)},
                device_id_type=MESH,
            )
            copy.start()
            copies.append(copy)
        if phase == 0:
            last = iters % 2
            out_ref[0] = field[last, inner_x, inner_y]
        for copy in copies:
            copy.wait()
        total = red[phase, 0]
        for d in range(1, count):
            total = total + red[phase, d]
        acc[...] = total
    share = jnp.sum(acc[...], axis=(0, 1), keepdims=True) * (1.0 / (iters * nrec))
    misfit_ref[...] = jnp.broadcast_to(share, misfit_ref.shape)


def local(
    sizes,
    velocity,
    direction,
    wave_prev,
    wave_now,
    winner,
    step_lengths,
    src_cell,
    wavelet,
    rec_cells,
    observed,
):
    trials, tiles_x, tiles_y = sizes
    cells_x, cells_y, depth = velocity.shape[1:]
    iters, nrec = observed.shape
    if trials != 2:
        root = winner[0] % trials
        velocity = from_root(velocity, "trial", root)
        direction = from_root(direction, "trial", root)
    plane = cells_y * tiles_y * depth
    rec_x = rec_cells // plane - lax.axis_index("tx") * cells_x
    rec_y = rec_cells % plane // depth - lax.axis_index("ty") * cells_y
    inside = (rec_x >= 0) & (rec_x < cells_x) & (rec_y >= 0) & (rec_y < cells_y)
    rec_row = jnp.where(inside, rec_x * cells_y + rec_y, -1).reshape(1, nrec)
    rec_z = jnp.where(inside, rec_cells % depth, -1).reshape(1, nrec)
    vmem = pl.BlockSpec(memory_space=pltpu.VMEM)
    smem = pl.BlockSpec(memory_space=pltpu.SMEM)
    block = (cells_x, cells_y, depth)
    faces = (2, 2, HALO, cells_x, depth)
    most = max(tiles_x, tiles_y)
    out, misfit = pl.pallas_call(
        functools.partial(kernel, sizes),
        out_shape=(
            jax.ShapeDtypeStruct((1,) + block, jnp.float32),
            jax.ShapeDtypeStruct((1, 128), jnp.float32),
        ),
        in_specs=[vmem] * 4 + [smem] * 4 + [vmem] * 3,
        out_specs=(vmem, vmem),
        scratch_shapes=[
            pltpu.VMEM((2, cells_x + 2 * HALO, cells_y + 2 * PAD, depth), jnp.float32),
            pltpu.VMEM(block, jnp.float32),
            pltpu.VMEM(block, jnp.float32),
            pltpu.VMEM(block, jnp.float32),
            pltpu.VMEM(faces, jnp.float32),
            pltpu.VMEM(faces, jnp.float32),
            pltpu.VMEM((nrec // CHUNK, cells_x * cells_y, CHUNK), jnp.bfloat16),
            pltpu.VMEM((3 * depth, cells_x * cells_y), jnp.bfloat16),
            pltpu.VMEM((8, 128), jnp.float32),
            pltpu.VMEM((2, most, 8, 128), jnp.float32),
            pltpu.SemaphoreType.DMA((2, 2)),
            pltpu.SemaphoreType.DMA((2, 2)),
            pltpu.SemaphoreType.DMA((2, 2)),
            pltpu.SemaphoreType.DMA((2, 2)),
            pltpu.SemaphoreType.DMA,
            pltpu.SemaphoreType.DMA,
            pltpu.SemaphoreType.DMA((2, most)),
            pltpu.SemaphoreType.DMA((2, most)),
        ],
        compiler_params=pltpu.CompilerParams(
            collective_id=0, has_side_effects=True, vmem_limit_bytes=40 * 1024 * 1024
        ),
    )(
        velocity,
        direction,
        wave_prev,
        wave_now,
        winner,
        step_lengths,
        src_cell,
        wavelet,
        rec_row,
        rec_z,
        observed,
    )
    return out, misfit[0, :1]


def solution(mesh):
    sizes = tuple(mesh.shape[axis] for axis in ("trial", "tx", "ty"))
    spread = P("trial", "tx", "ty", None)
    return jax.shard_map(
        functools.partial(local, sizes),
        mesh=mesh,
        in_specs=(spread,) * 4 + (P(),) * 6,
        out_specs=(spread, P("trial")),
        check_vma=False,
    )
```

time: 342 us -> 72.7 us (0.21)
  local copies, waits for them, and re-layouts: 112 us -> 6.27 us
  starting transfers between devices: 95.8 us -> 0 us
  Pallas kernels: 0 us -> 61.4 us
  between operations: 43 us -> 3.17 us
  blocking collectives: 35.5 us -> 0 us
  waiting for transfers between devices: 34.7 us -> 0 us
  other arithmetic: 18.6 us -> 1.44 us
    ppermute x32 -> x0, starting transfers between devices: 95.7 us -> none  [the longest x16 74.9 us: extended(): lax.ppermute(lax.slice_in_dim(block, block.shape[dim] - width, None, axis...]
    gather x8 -> x0, local copies, waits for them, and re-layouts: 94.3 us -> none  [local(): picked = jnp.take(nxt.reshape(-1), rec_local)]
    pallas_call x0 -> x1, Pallas kernels: none -> 61.4 us  [local(): pl.pallas_call(functools.partial(kernel, sizes), out_shape=(jax.ShapeDtyp...]
    psum x1 -> x0, blocking collectives: 35.5 us -> none  [local(): summed = lax.psum(total, ('tx', 'ty'))]
    psum x1 -> x0, waiting for transfers between devices: 23.7 us -> none  [from_root(): return lax.psum(block, axis)]
    add x16 -> x0, other arithmetic: 15 us -> none  [the longest x8 7.71 us: advance(): nxt = 2.0 * now_pad[2:-2, 2:-2] - prev_ext + speed_ext * lap]
    ppermute x32 -> x0, waiting for transfers between devices: 11 us -> none  [the longest x16 11 us: extended(): lax.ppermute(lax.slice_in_dim(block, block.shape[dim] - width, None, axis...]
    another operation x8 -> x0, local copies, waits for them, and re-layouts: 6.71 us -> none
  transfers between devices with their start and end apart: 33 -> 0, of which waited for: 14 -> 0; matrix products, arithmetic and copies ran while one was open for 25% -> 0% of each run, Pallas kernels for 0% -> 0%
where the time goes in v1:
time: 72.7 us; the launch traced here: 72.3 us
  Pallas kernels  61.4 us (84%)
  local copies, waits for them, and re-layouts  6.27 us (9%)
  between operations  3.17 us (4%)
  other arithmetic  1.44 us (2%)
    pallas_call x1, Pallas kernels, local(): pl.pallas_call(functools.partial(kernel, sizes), out_shape=(jax.ShapeDtyp...  61.4 us
    unnamed x15, local copies, waits for them, and re-layouts  6.27 us

profile of v1, /device:TPU:0, one launch (start us, length us, event | category | flops | bytes accessed | tf_op | source)
XLA Modules:
  0.0 72.3 jit_solution(15156228661955100049)
XLA Ops:
  0.6 0.0 copy-start.4
  2.0 0.7 fusion.3
  2.7 0.7 add_select_fusion.4
  3.4 0.0 copy-done.4
  3.4 0.0 copy-start
  3.4 1.0 %copy-done = f32[1,16,64,128]{3,2,1,0:T(8,128)S(1)} copy-done((f32[1,16,64,128]{3,2,1,0:T(8,128)S(1)}, f32[1,16,64,128]{3,2,1,0:T(8,128)}, u32[]{:S(2)}) %copy-start) | copy-done | bytes 524312
  4.5 0.0 copy-start.1
  4.5 1.0 %copy-done.1 = f32[1,16,64,128]{3,2,1,0:T(8,128)S(1)} copy-done((f32[1,16,64,128]{3,2,1,0:T(8,128)S(1)}, f32[1,16,64,128]{3,2,1,0:T(8,128)}, u32[]{:S(2)}) %copy-start.1) | copy-done | bytes 524312
  5.5 0.0 copy-start.2
  5.5 1.0 %copy-done.2 = f32[1,16,64,128]{3,2,1,0:T(8,128)S(1)} copy-done((f32[1,16,64,128]{3,2,1,0:T(8,128)S(1)}, f32[1,16,64,128]{3,2,1,0:T(8,128)}, u32[]{:S(2)}) %copy-start.2) | copy-done | bytes 524312
  6.6 0.0 copy-start.3
  6.6 1.0 %copy-done.3 = f32[1,16,64,128]{3,2,1,0:T(8,128)S(1)} copy-done((f32[1,16,64,128]{3,2,1,0:T(8,128)S(1)}, f32[1,16,64,128]{3,2,1,0:T(8,128)}, u32[]{:S(2)}) %copy-start.3) | copy-done | bytes 524312
  7.6 0.0 copy-start.5
  7.6 0.7 copy-done.5
  8.3 0.0 copy-start.6
  8.3 0.7 copy-done.6
  8.9 61.4 %shard_map.113 = (f32[1,16,64,128]{3,2,1,0:T(8,128)S(1)}, f32[1,128]{1,0:T(1,128)S(1)}) custom-call(f32[1,16,64,128]{3,2,1,0:T(8,128)S(1)} %copy-done, f32[1,16,64,128]{3,2,1,0:T(8,128)S(1)} %copy-done.1, f32[1,16,64,128]{3,2,1,0:T(8,128)S(1)} %copy-done.2, f32[1,16,64,128]{3,2,1,0:T(8,128)S(1)} %copy-done.3, s32[1]{0:T(128)S(6)} %copy.14.winner_ref, ...), custom_call_target="tpu_custom_call" | custom-call | tf_op jit(solution)/shard_map/pallas_call | solution.py:358
  70.3 0.8 %copy.16 = f32[1,16,64,128]{3,2,1,0:T(8,128)} copy(f32[1,16,64,128]{3,2,1,0:T(8,128)S(1)} %get-tuple-element.10) | data formatting | bytes 1048576
Async XLA Ops:
  0.6 2.8 %copy-start.4 = (f32[8,2048]{1,0:T(8,128)S(1)}, f32[8,2048]{1,0:T(8,128)}, u32[]{:S(2)}) copy-start(f32[8,2048]{1,0:T(8,128)} %obs_ref.1) | copy-start | bytes 196612
  3.4 1.0 %copy-start = (f32[1,16,64,128]{3,2,1,0:T(8,128)S(1)}, f32[1,16,64,128]{3,2,1,0:T(8,128)}, u32[]{:S(2)}) copy-start(f32[1,16,64,128]{3,2,1,0:T(8,128)} %vel_ref.1) | copy-start | bytes 1572868
  4.5 1.0 %copy-start.1 = (f32[1,16,64,128]{3,2,1,0:T(8,128)S(1)}, f32[1,16,64,128]{3,2,1,0:T(8,128)}, u32[]{:S(2)}) copy-start(f32[1,16,64,128]{3,2,1,0:T(8,128)} %dir_ref.1) | copy-start | bytes 1572868
  5.5 1.0 %copy-start.2 = (f32[1,16,64,128]{3,2,1,0:T(8,128)S(1)}, f32[1,16,64,128]{3,2,1,0:T(8,128)}, u32[]{:S(2)}) copy-start(f32[1,16,64,128]{3,2,1,0:T(8,128)} %prev_ref.1) | copy-start | bytes 1572868
  6.6 1.0 %copy-start.3 = (f32[1,16,64,128]{3,2,1,0:T(8,128)S(1)}, f32[1,16,64,128]{3,2,1,0:T(8,128)}, u32[]{:S(2)}) copy-start(f32[1,16,64,128]{3,2,1,0:T(8,128)} %now_ref.1) | copy-start | bytes 1572868
  7.6 0.7 copy-start.5
  8.3 0.7 copy-start.6

commit v2 on v1

v2 whole, which is shorter than its diff:
```python
import functools

import jax
import jax.numpy as jnp
from jax import lax
from jax.experimental import pallas as pl
from jax.experimental.pallas import tpu as pltpu
from jax.sharding import PartitionSpec as P

MESH = pl.DeviceIdType.MESH
coef_mid = -2.5
coef_one = 4.0 / 3.0
coef_two = -1.0 / 12.0
dt_over_h = 0.1
HALO = 2
PAD = 8
CHUNK = 256
PLANES = 4
PARTS = 2


def quotient(value, by):
    if by & (by - 1) == 0:
        return lax.shift_right_logical(value, jnp.full_like(value, by.bit_length() - 1))
    return lax.div(value, jnp.full_like(value, by))


def parts(value):
    pieces = []
    for _ in range(PARTS):
        piece = value.astype(jnp.bfloat16)
        pieces.append(piece)
        value = value - piece.astype(jnp.float32)
    return pieces


def from_root(block, axis, source):
    block = jnp.where(lax.axis_index(axis) == source, block, jnp.zeros_like(block))
    return lax.psum(block, axis)


def kernel(
    sizes,
    vel_ref,
    dir_ref,
    prev_ref,
    now_ref,
    winner_ref,
    steps_ref,
    src_ref,
    wavelet_ref,
    rec_hbm,
    obs_hbm,
    out_ref,
    misfit_ref,
    field,
    rec_z,
    speed,
    speed_out,
    speed_in,
    y_out,
    y_in,
    hot,
    lhs,
    acc,
    red,
    x_send,
    x_recv,
    y_send,
    y_recv,
    sp_send,
    sp_recv,
    red_send,
    red_recv,
    vel,
    head,
    in_sem,
    wave_sem,
    out_sem,
    rec_ref,
    obs_ref,
    band,
    data_sem,
):
    trials, tiles_x, tiles_y = sizes
    cells_x, cells_y, depth = now_ref.shape[1:]
    groups = cells_x // PLANES
    iters, nrec = obs_hbm.shape
    exchange = trials == 2
    k = lax.axis_index("trial")
    ix = lax.axis_index("tx")
    iy = lax.axis_index("ty")
    inner_x = pl.ds(HALO, cells_x)
    inner_y = pl.ds(PAD, cells_y)

    loads = []
    for g in range(groups):
        some = pl.ds(g * PLANES, PLANES)
        pair = (
            pltpu.make_async_copy(vel_ref.at[0, some], vel.at[some], in_sem.at[0, g]),
            pltpu.make_async_copy(dir_ref.at[0, some], head.at[some], in_sem.at[1, g]),
        )
        for load in pair:
            load.start()
        loads.append(pair)
    waves = (
        pltpu.make_async_copy(now_ref.at[0], field.at[0, inner_x, inner_y], wave_sem.at[0]),
        pltpu.make_async_copy(prev_ref.at[0], field.at[1, inner_x, inner_y], wave_sem.at[1]),
    )
    data = (
        pltpu.make_async_copy(rec_hbm, rec_ref, data_sem.at[0]),
        pltpu.make_async_copy(obs_hbm, obs_ref, data_sem.at[1]),
    )
    for load in waves + data:
        load.start()

    for slot in range(2):
        for x in (0, 1, HALO + cells_x, HALO + cells_x + 1):
            field[slot, x] = jnp.zeros(field.shape[2:], jnp.float32)
        field[slot, inner_x, pl.ds(0, PAD)] = jnp.zeros((cells_x, PAD, depth), jnp.float32)
        field[slot, inner_x, pl.ds(PAD + cells_y, PAD)] = jnp.zeros(
            (cells_x, PAD, depth), jnp.float32
        )

    peers = [
        {"tx": lax.rem(ix + dx, tiles_x), "ty": lax.rem(iy + dy, tiles_y)}
        for dx in range(tiles_x)
        for dy in range(tiles_y)
    ]
    greet = peers[1:] + ([{"trial": 1 - k}] if exchange else [])
    barrier = pltpu.get_barrier_semaphore()
    for peer in greet:
        pl.semaphore_signal(barrier, inc=1, device_id=peer, device_id_type=MESH)

    mine = steps_ref[k]
    if exchange:
        other = steps_ref[1 - k]

    def speed_copy(g):
        some = pl.ds(g * PLANES, PLANES)
        return pltpu.make_async_remote_copy(
            src_ref=speed_out.at[some],
            dst_ref=speed_in.at[some],
            send_sem=sp_send.at[g],
            recv_sem=sp_recv.at[g],
            device_id={"trial": 1 - k},
            device_id_type=MESH,
        )

    for g in range(groups):
        for load in loads[g]:
            load.wait()
        some = pl.ds(g * PLANES, PLANES)
        v, d = vel[some], head[some]
        if exchange:
            far = (v + other * d) * dt_over_h
            speed_out[some] = far * far
        own = (v + mine * d) * dt_over_h
        speed[some] = own * own
        if g == 0 and greet:
            pl.semaphore_wait(barrier, len(greet))
        if exchange:
            speed_copy(g).start()
    for load in waves:
        load.wait()

    def x_copy(slot, side):
        src = HALO if side == 0 else cells_x
        dst = HALO + cells_x if side == 0 else 0
        to = jnp.maximum(ix - 1, 0) if side == 0 else jnp.minimum(ix + 1, tiles_x - 1)
        return pltpu.make_async_remote_copy(
            src_ref=field.at[slot, pl.ds(src, HALO), inner_y],
            dst_ref=field.at[slot, pl.ds(dst, HALO), inner_y],
            send_sem=x_send.at[slot, side],
            recv_sem=x_recv.at[slot, side],
            device_id={"tx": to},
            device_id_type=MESH,
        )

    def y_copy(slot, side):
        to = jnp.maximum(iy - 1, 0) if side == 0 else jnp.minimum(iy + 1, tiles_y - 1)
        return pltpu.make_async_remote_copy(
            src_ref=y_out.at[slot, side],
            dst_ref=y_in.at[slot, side],
            send_sem=y_send.at[slot, side],
            recv_sem=y_recv.at[slot, side],
            device_id={"ty": to},
            device_id_type=MESH,
        )

    below_x, above_x = ix > 0, ix < tiles_x - 1
    below_y, above_y = iy > 0, iy < tiles_y - 1

    def send_x(slot):
        @pl.when(below_x)
        def _():
            x_copy(slot, 0).start()

        @pl.when(above_x)
        def _():
            x_copy(slot, 1).start()

    def send_y(slot):
        for j in range(HALO):
            y_out[slot, 0, j] = field[slot, inner_x, PAD + j, :]
            y_out[slot, 1, j] = field[slot, inner_x, PAD + cells_y - HALO + j, :]

        @pl.when(below_y)
        def _():
            y_copy(slot, 0).start()

        @pl.when(above_y)
        def _():
            y_copy(slot, 1).start()

    def take_faces(slot):
        @pl.when(below_x)
        def _():
            x_copy(slot, 1).wait_recv()
            x_copy(slot, 0).wait_send()

        @pl.when(above_x)
        def _():
            x_copy(slot, 0).wait_recv()
            x_copy(slot, 1).wait_send()

        @pl.when(below_y)
        def _():
            y_copy(slot, 1).wait_recv()
            y_copy(slot, 0).wait_send()
            for j in range(HALO):
                field[slot, inner_x, PAD - HALO + j, :] = y_in[slot, 1, j]

        @pl.when(above_y)
        def _():
            y_copy(slot, 0).wait_recv()
            y_copy(slot, 1).wait_send()
            for j in range(HALO):
                field[slot, inner_x, PAD + cells_y + j, :] = y_in[slot, 0, j]

    send_x(0)
    send_y(0)
    rows = cells_x * cells_y
    step_rows = 256 if rows % 256 == 0 else rows
    whole_y = cells_y * tiles_y
    for load in data:
        load.wait()
    cell = rec_ref[...]
    rec_x = quotient(cell, whole_y * depth)
    rec_y = quotient(cell - rec_x * (whole_y * depth), depth)
    z = cell - (rec_x * whole_y + rec_y) * depth
    rec_x = rec_x - ix * cells_x
    rec_y = rec_y - iy * cells_y
    inside = (rec_x >= 0) & (rec_x < cells_x) & (rec_y >= 0) & (rec_y < cells_y)
    rec_row = jnp.where(inside, rec_x * cells_y + rec_y, -1)
    rec_z[...] = jnp.where(inside, z, -1)
    for c in range(nrec // CHUNK):
        at = rec_row[:, c * CHUNK : (c + 1) * CHUNK]

        def mark(b, _, c=c, at=at):
            row = lax.broadcasted_iota(jnp.int32, (step_rows, CHUNK), 0) + b * step_rows
            start = pl.multiple_of(b * step_rows, step_rows)
            hot[c, pl.ds(start, step_rows)] = jnp.where(row == at, 1.0, 0.0).astype(jnp.bfloat16)
            return 0

        lax.fori_loop(0, rows // step_rows, mark, 0)
    acc[...] = jnp.zeros_like(acc)

    flat = src_ref[0]
    src_x = lax.div(flat, whole_y * depth) - ix * cells_x
    in_plane = lax.rem(flat, whole_y * depth)
    src_y = lax.div(in_plane, depth) - iy * cells_y
    src_yz = jnp.where(
        (src_y >= 0) & (src_y < cells_y), src_y * depth + lax.rem(in_plane, depth), -1
    )

    plane = (cells_y, depth)
    place = lax.broadcasted_iota(jnp.int32, plane, 0) * depth
    place = place + lax.broadcasted_iota(jnp.int32, plane, 1)
    source = lax.broadcasted_iota(jnp.int32, (depth, depth), 0)
    target = lax.broadcasted_iota(jnp.int32, (depth, depth), 1)
    apart = jnp.abs(source - target)
    for reach in (1, 2):
        ones = jnp.where(apart == reach, 1.0, 0.0).astype(jnp.bfloat16)
        for part in range(PARTS):
            band[part * depth : (part + 1) * depth, (reach - 1) * depth : reach * depth] = ones

    who = jnp.full(plane, lax.rem(winner_ref[0], trials), jnp.int32)
    keep = who == k
    result = pltpu.make_async_copy(
        field.at[iters % 2, inner_x, inner_y], out_ref.at[0], out_sem
    )

    def step(t, _):
        slot = lax.rem(t, 2)
        late = 1 - slot
        take_faces(slot)
        amp = wavelet_ref[t]

        def advance(x, near_z, far_z):
            u = field[slot, x + HALO, inner_y]
            total = (3.0 * coef_mid) * u
            near = field[slot, x + 3, inner_y] + field[slot, x + 1, inner_y]
            far = field[slot, x + 4, inner_y] + field[slot, x, inner_y]
            near = near + (
                field[slot, x + HALO, pl.ds(PAD + 1, cells_y)]
                + field[slot, x + HALO, pl.ds(PAD - 1, cells_y)]
            )
            far = far + (
                field[slot, x + HALO, pl.ds(PAD + 2, cells_y)]
                + field[slot, x + HALO, pl.ds(PAD - 2, cells_y)]
            )
            total = total + coef_one * (near + near_z) + coef_two * (far + far_z)
            here = jnp.where(src_x == x, src_yz, -1)
            total = total + jnp.where(place == here, amp, 0.0)
            prev = field[late, x + HALO, inner_y]
            field[late, x + HALO, inner_y] = 2.0 * u - prev + speed[x] * total

        def advance_some(g, _):
            if exchange:

                @pl.when(t == 0)
                def _():
                    speed_copy(g).wait()
                    for i in range(PLANES):
                        x = g * PLANES + i
                        speed[x] = jnp.where(keep, speed[x], speed_in[x])

            some = field[slot, pl.ds(HALO + g * PLANES, PLANES), inner_y]
            along = jnp.dot(
                jnp.concatenate(parts(some.reshape(PLANES * cells_y, depth)), axis=1),
                band[...],
                preferred_element_type=jnp.float32,
            )
            for i in range(PLANES):
                lines = along[i * cells_y : (i + 1) * cells_y]
                advance(g * PLANES + i, lines[:, :depth], lines[:, depth:])

        for g in sorted({0, groups - 1}):
            advance_some(g, 0)

        @pl.when(t < iters - 1)
        def _():
            send_x(late)

        for g in range(1, groups - 1):
            advance_some(g, 0)

        @pl.when(t < iters - 1)
        def _():
            send_y(late)

        @pl.when(t == iters - 1)
        def _():
            result.start()

        pair = max(1, 128 // cells_y)
        wide = pair * cells_y
        for p in range(cells_x // pair):
            block = field[late, pl.ds(HALO + p * pair, pair), inner_y]
            turned = block.reshape(wide, depth).T
            for part, piece in enumerate(parts(turned)):
                lhs[part * depth : (part + 1) * depth, p * wide : (p + 1) * wide] = piece
        zs = lax.broadcasted_iota(jnp.int32, (depth, CHUNK), 0)
        for c in range(nrec // CHUNK):
            got = jnp.dot(lhs[...], hot[c], preferred_element_type=jnp.float32)
            picked = got[:depth]
            for part in range(1, PARTS):
                picked = picked + got[part * depth : (part + 1) * depth]
            cols = pl.ds(c * CHUNK, CHUNK)
            gap = picked - obs_ref[pl.ds(t, 1), cols]
            part = jnp.where(zs == rec_z[:, cols], gap * gap, 0.0)
            part = part.reshape(depth // 8, 8, CHUNK).sum(axis=0)
            acc[...] += part[:, :128] + part[:, 128:]
        return 0

    lax.fori_loop(0, iters, step, 0)

    copies = []
    for d in range(1, len(peers)):
        copy = pltpu.make_async_remote_copy(
            src_ref=acc,
            dst_ref=red.at[d],
            send_sem=red_send.at[d],
            recv_sem=red_recv.at[d],
            device_id=peers[d],
            device_id_type=MESH,
        )
        copy.start()
        copies.append(copy)
    total = acc[...]
    for d, copy in enumerate(copies, 1):
        copy.wait()
        total = total + red[d]
    result.wait()
    share = jnp.sum(total, axis=(0, 1), keepdims=True) * (1.0 / (iters * nrec))
    misfit_ref[...] = jnp.broadcast_to(share, misfit_ref.shape)


def local(
    sizes,
    velocity,
    direction,
    wave_prev,
    wave_now,
    winner,
    step_lengths,
    src_cell,
    wavelet,
    rec_cells,
    observed,
):
    trials, tiles_x, tiles_y = sizes
    cells_x, cells_y, depth = velocity.shape[1:]
    iters, nrec = observed.shape
    if trials != 2:
        root = winner[0] % trials
        velocity = from_root(velocity, "trial", root)
        direction = from_root(direction, "trial", root)
    vmem = pl.BlockSpec(memory_space=pltpu.VMEM)
    smem = pl.BlockSpec(memory_space=pltpu.SMEM)
    block = (cells_x, cells_y, depth)
    faces = (2, 2, HALO, cells_x, depth)
    tiles = tiles_x * tiles_y
    groups = cells_x // PLANES
    whole = pl.BlockSpec(memory_space=pltpu.HBM)
    out, misfit = pl.pallas_call(
        functools.partial(kernel, sizes),
        out_shape=(
            jax.ShapeDtypeStruct((1,) + block, jnp.float32),
            jax.ShapeDtypeStruct((1, 128), jnp.float32),
        ),
        in_specs=[whole] * 4 + [smem] * 4 + [whole] * 2,
        out_specs=(whole, vmem),
        scratch_shapes=[
            pltpu.VMEM((2, cells_x + 2 * HALO, cells_y + 2 * PAD, depth), jnp.float32),
            pltpu.VMEM((1, nrec), jnp.int32),
            pltpu.VMEM(block, jnp.float32),
            pltpu.VMEM(block, jnp.float32),
            pltpu.VMEM(block, jnp.float32),
            pltpu.VMEM(faces, jnp.float32),
            pltpu.VMEM(faces, jnp.float32),
            pltpu.VMEM((nrec // CHUNK, cells_x * cells_y, CHUNK), jnp.bfloat16),
            pltpu.VMEM((PARTS * depth, cells_x * cells_y), jnp.bfloat16),
            pltpu.VMEM((8, 128), jnp.float32),
            pltpu.VMEM((tiles, 8, 128), jnp.float32),
            pltpu.SemaphoreType.DMA((2, 2)),
            pltpu.SemaphoreType.DMA((2, 2)),
            pltpu.SemaphoreType.DMA((2, 2)),
            pltpu.SemaphoreType.DMA((2, 2)),
            pltpu.SemaphoreType.DMA((groups,)),
            pltpu.SemaphoreType.DMA((groups,)),
            pltpu.SemaphoreType.DMA((tiles,)),
            pltpu.SemaphoreType.DMA((tiles,)),
            pltpu.VMEM(block, jnp.float32),
            pltpu.VMEM(block, jnp.float32),
            pltpu.SemaphoreType.DMA((2, groups)),
            pltpu.SemaphoreType.DMA((2,)),
            pltpu.SemaphoreType.DMA,
            pltpu.VMEM((1, nrec), jnp.int32),
            pltpu.VMEM((iters, nrec), jnp.float32),
            pltpu.VMEM((PARTS * depth, 2 * depth), jnp.bfloat16),
            pltpu.SemaphoreType.DMA((2,)),
        ],
        compiler_params=pltpu.CompilerParams(
            collective_id=0, has_side_effects=True, vmem_limit_bytes=62 * 1024 * 1024
        ),
    )(
        velocity,
        direction,
        wave_prev,
        wave_now,
        winner,
        step_lengths,
        src_cell,
        wavelet,
        rec_cells.reshape(1, nrec),
        observed,
    )
    return out, misfit[0, :1]


def solution(mesh):
    sizes = tuple(mesh.shape[axis] for axis in ("trial", "tx", "ty"))
    spread = P("trial", "tx", "ty", None)
    return jax.shard_map(
        functools.partial(local, sizes),
        mesh=mesh,
        in_specs=(spread,) * 4 + (P(),) * 6,
        out_specs=(spread, P("trial")),
        check_vma=False,
    )
```

time: 72.7 us -> 60.6 us (0.83)
  Pallas kernels: 61.4 us -> 55.4 us
  local copies, waits for them, and re-layouts: 6.27 us -> 1.89 us
  other arithmetic: 1.44 us -> 0 us
    pallas_call x1, Pallas kernels: 61.4 us -> 55.4 us  [local(): pl.pallas_call(functools.partial(kernel, sizes), out_shape=(jax.ShapeDtyp...]
    unnamed x15 -> x3, local copies, waits for them, and re-layouts: 6.27 us -> 1.89 us
    select_n x2 -> x0, other arithmetic: 1.44 us -> none  [the longest x1 0.72 us: local(): rec_z = jnp.where(inside, rec_cells % depth, -1).reshape(1, nrec)]
where the time goes in v2:
time: 60.6 us; the launch traced here: 60.4 us
  Pallas kernels  55.4 us (91%)
  between operations  3.11 us (5%)
  local copies, waits for them, and re-layouts  1.89 us (3%)
    pallas_call x1, Pallas kernels, local(): pl.pallas_call(functools.partial(kernel, sizes), out_shape=(jax.ShapeDtyp...  55.4 us
    unnamed x3, local copies, waits for them, and re-layouts  1.89 us

profile of v2, /device:TPU:0, one launch (start us, length us, event | category | flops | bytes accessed | tf_op | source)
XLA Modules:
  0.0 60.4 jit_solution(10838234784450710503)
XLA Ops:
  1.9 55.4 %shard_map.113 = (f32[1,16,64,128]{3,2,1,0:T(8,128)}, f32[1,128]{1,0:T(1,128)}) custom-call(f32[1,16,64,128]{3,2,1,0:T(8,128)} %vel_ref.1, f32[1,16,64,128]{3,2,1,0:T(8,128)} %dir_ref.1, f32[1,16,64,128]{3,2,1,0:T(8,128)} %prev_ref.1, f32[1,16,64,128]{3,2,1,0:T(8,128)} %now_ref.1, s32[1]{0:T(128)S(6)} %copy.14.winner_ref, f32[2]{0:T(128)} %steps_ref.1, ...), custom_call_target="tpu_custom_call" | custom-call | tf_op jit(solution)/shard_map/pallas_call | solution.py:427
  57.3 0.0 copy-start
  57.3 1.9 %copy.16 = f32[1,16,64,128]{3,2,1,0:T(8,128)} copy(f32[1,16,64,128]{3,2,1,0:T(8,128)} %get-tuple-element.8) | data formatting | bytes 1048576
  59.2 0.0 copy-done
Async XLA Ops:
  57.3 1.9 %copy-start = (f32[1,128]{1,0:T(1,128)S(1)}, f32[1,128]{1,0:T(1,128)}, u32[]{:S(2)}) copy-start(f32[1,128]{1,0:T(1,128)} %get-tuple-element.5) | copy-start | bytes 1540

commit v3 on v2

--- a/solution.py
+++ b/solution.py
@@ -297,58 +297,63 @@
         take_faces(slot)
         amp = wavelet_ref[t]
 
-        def advance(x, near_z, far_z):
-            u = field[slot, x + HALO, inner_y]
+        def advance(x, row, count, near_z, far_z):
+            part_y = pl.ds(PAD + row, count)
+            u = field[slot, x + HALO, part_y]
             total = (3.0 * coef_mid) * u
-            near = field[slot, x + 3, inner_y] + field[slot, x + 1, inner_y]
-            far = field[slot, x + 4, inner_y] + field[slot, x, inner_y]
+            near = field[slot, x + 3, part_y] + field[slot, x + 1, part_y]
+            far = field[slot, x + 4, part_y] + field[slot, x, part_y]
             near = near + (
-                field[slot, x + HALO, pl.ds(PAD + 1, cells_y)]
-                + field[slot, x + HALO, pl.ds(PAD - 1, cells_y)]
+                field[slot, x + HALO, pl.ds(PAD + row + 1, count)]
+                + field[slot, x + HALO, pl.ds(PAD + row - 1, count)]
             )
             far = far + (
-                field[slot, x + HALO, pl.ds(PAD + 2, cells_y)]
-                + field[slot, x + HALO, pl.ds(PAD - 2, cells_y)]
+                field[slot, x + HALO, pl.ds(PAD + row + 2, count)]
+                + field[slot, x + HALO, pl.ds(PAD + row - 2, count)]
             )
             total = total + coef_one * (near + near_z) + coef_two * (far + far_z)
             here = jnp.where(src_x == x, src_yz, -1)
-            total = total + jnp.where(place == here, amp, 0.0)
-            prev = field[late, x + HALO, inner_y]
-            field[late, x + HALO, inner_y] = 2.0 * u - prev + speed[x] * total
-
-        def advance_some(g, _):
-            if exchange:
-
-                @pl.when(t == 0)
-                def _():
+            total = total + jnp.where(place[row : row + count] == here, amp, 0.0)
+            prev = field[late, x + HALO, part_y]
+            field[late, x + HALO, part_y] = 2.0 * u - prev + speed[x, pl.ds(row, count)] * total
+
+        def advance_some(first, planes, row, count):
+            some = field[slot, pl.ds(HALO + first, planes), pl.ds(PAD + row, count)]
+            along = jnp.dot(
+                jnp.concatenate(parts(some.reshape(planes * count, depth)), axis=1),
+                band[...],
+                preferred_element_type=jnp.float32,
+            )
+            for i in range(planes):
+                lines = along[i * count : (i + 1) * count]
+                advance(first + i, row, count, lines[:, :depth], lines[:, depth:])
+
+        if exchange:
+
+            @pl.when(t == 0)
+            def _():
+                for g in range(groups):
                     speed_copy(g).wait()
                     for i in range(PLANES):
                         x = g * PLANES + i
                         speed[x] = jnp.where(keep, speed[x], speed_in[x])
 
-            some = field[slot, pl.ds(HALO + g * PLANES, PLANES), inner_y]
-            along = jnp.dot(
-                jnp.concatenate(parts(some.reshape(PLANES * cells_y, depth)), axis=1),
-                band[...],
-                preferred_element_type=jnp.float32,
-            )
-            for i in range(PLANES):
-                lines = along[i * cells_y : (i + 1) * cells_y]
-                advance(g * PLANES + i, lines[:, :depth], lines[:, depth:])
+        for row in (0, cells_y - PAD):
+            advance_some(0, cells_x, row, PAD)
+
+        @pl.when(t < iters - 1)
+        def _():
+            send_y(late)
 
         for g in sorted({0, groups - 1}):
-            advance_some(g, 0)
+            advance_some(g * PLANES, PLANES, PAD, cells_y - 2 * PAD)
 
         @pl.when(t < iters - 1)
         def _():
             send_x(late)
 
         for g in range(1, groups - 1):
-            advance_some(g, 0)
-
-        @pl.when(t < iters - 1)
-        def _():
-            send_y(late)
+            advance_some(g * PLANES, PLANES, PAD, cells_y - 2 * PAD)
 
         @pl.when(t == iters - 1)
         def _():

time: 60.6 us -> 57.3 us (0.946)
  Pallas kernels: 55.4 us -> 52.1 us
    pallas_call x1, Pallas kernels: 55.4 us -> 52.1 us  [local(): pl.pallas_call(functools.partial(kernel, sizes), out_shape=(jax.ShapeDtyp...]
where the time goes in v3:
time: 57.3 us; the launch traced here: 57.1 us
  Pallas kernels  52.1 us (91%)
  between operations  3.11 us (5%)
  local copies, waits for them, and re-layouts  1.89 us (3%)
    pallas_call x1, Pallas kernels, local(): pl.pallas_call(functools.partial(kernel, sizes), out_shape=(jax.ShapeDtyp...  52.1 us
    unnamed x3, local copies, waits for them, and re-layouts  1.89 us

profile of v3, /device:TPU:0, one launch (start us, length us, event | category | flops | bytes accessed | tf_op | source)
XLA Modules:
  0.0 57.1 jit_solution(17615589140419236636)
XLA Ops:
  1.9 52.1 %shard_map.113 = (f32[1,16,64,128]{3,2,1,0:T(8,128)}, f32[1,128]{1,0:T(1,128)}) custom-call(f32[1,16,64,128]{3,2,1,0:T(8,128)} %vel_ref.1, f32[1,16,64,128]{3,2,1,0:T(8,128)} %dir_ref.1, f32[1,16,64,128]{3,2,1,0:T(8,128)} %prev_ref.1, f32[1,16,64,128]{3,2,1,0:T(8,128)} %now_ref.1, s32[1]{0:T(128)S(6)} %copy.14.winner_ref, f32[2]{0:T(128)} %steps_ref.1, ...), custom_call_target="tpu_custom_call" | custom-call | tf_op jit(solution)/shard_map/pallas_call | solution.py:432
  54.0 0.0 copy-start
  54.0 1.9 %copy.16 = f32[1,16,64,128]{3,2,1,0:T(8,128)} copy(f32[1,16,64,128]{3,2,1,0:T(8,128)} %get-tuple-element.8) | data formatting | bytes 1048576
  55.9 0.0 copy-done
Async XLA Ops:
  54.0 1.9 %copy-start = (f32[1,128]{1,0:T(1,128)S(1)}, f32[1,128]{1,0:T(1,128)}, u32[]{:S(2)}) copy-start(f32[1,128]{1,0:T(1,128)} %get-tuple-element.5) | copy-start | bytes 1540
